TPU v7x, 32 devices: a whole 2x2x4 slice. The times are simulated.
32 devices in a mesh: tok: 8 (over y, x, core), rep: 4 (over z).
Axes of the slice: x: 2, y: 2, z: 4, core: 2. Of those that a mesh axis runs over, the one named last changes fastest.
Arguments:
- hidden_states: bfloat16 [4, 1024, 2048], P('rep', 'tok'), may hold values from -6 to 6
- routes: int32 [4, 1024, 8], P('rep', 'tok'), may hold values from 0 to 31, all different within a row; in each aligned block of 128 rows (0 to 127, 128 to 255, ..., all dimensions but the last counted through in order) at most 36 rows name the same one
- gate_prob: float32 [4, 1024, 8], P('rep', 'tok'), may hold values from 0.03 to 0.3
- gate_up: float32 [32, 2048, 2048], P('tok', 'rep'), may hold values from -0.125 to 0.125
- down: float32 [32, 1024, 2048], P('tok', 'rep'), may hold values from -0.1875 to 0.1875
Outputs:
- mixed: bfloat16 [4, 1024, 2048], P('rep', 'tok')
Inputs may be any that keep to these rules, and one draw needn't show every extreme that they name: `routes`: each row names 8 different experts. No expert is named by more than 36 rows of one device's 128 tokens, and some expert reaches 36 on some devices.
All inputs are finite; a program needn't handle non-finite values.
Results may differ from a plain program's by a relative error of at most 0.012.
Values may be sent and summed in bfloat16 or wider, within the bound.
A program may use at most 192 MiB of HBM per device.

v0:
```python
import jax
import jax.numpy as jnp
from jax import lax
from jax.sharding import PartitionSpec as P

CAP = 36


def per_device(hidden_states, routes, gate_prob, gate_up, down):
    groups = lax.axis_size("tok")
    local_experts = gate_up.shape[0]
    model_width = hidden_states.shape[2]
    token_count = hidden_states.shape[1]
    top_count = routes.shape[2]
    all_experts = groups * local_experts
    capacity = CAP
    served_gate = gate_up.astype(jnp.bfloat16)
    served_down = down.astype(jnp.bfloat16)
    unit_count = served_gate.shape[2] // 2
    full_gate, full_down = (
        lax.all_gather(served_gate, "rep", axis=1, tiled=True),
        lax.all_gather(served_down, "rep", axis=1, tiled=True),
    )
    flat_picks = routes[0].reshape(-1)
    pick_count = flat_picks.shape[0]
    one_hot = (flat_picks[:, None] == jnp.arange(all_experts, dtype=jnp.int32)[None, :]).astype(
        jnp.int32
    )
    earlier = jnp.cumsum(one_hot, axis=0) - one_hot
    slot_index = jnp.sum(earlier * one_hot, axis=1)
    owners = jnp.arange(pick_count, dtype=jnp.int32) // top_count
    slot_table = (
        jnp.full((all_experts, capacity), token_count, jnp.int32)
        .at[flat_picks, slot_index]
        .set(owners)
    )
    padded_rows = jnp.concatenate(
        [hidden_states[0], jnp.zeros((1, model_width), jnp.bfloat16)], axis=0
    )
    send_rows = padded_rows[slot_table].reshape(groups, local_experts, capacity, model_width)
    arrived = lax.all_to_all(send_rows, "tok", split_axis=0, concat_axis=0, tiled=True)
    gate_both = jnp.einsum("secd,edf->secf", arrived, full_gate, preferred_element_type=jnp.float32)
    hidden_units = (jax.nn.silu(gate_both[..., :unit_count]) * gate_both[..., unit_count:]).astype(
        jnp.bfloat16
    )
    projected = jnp.einsum(
        "secf,efd->secd", hidden_units, full_down, preferred_element_type=jnp.float32
    )
    expert_out = projected.astype(jnp.bfloat16)
    returned = lax.all_to_all(expert_out, "tok", split_axis=0, concat_axis=0, tiled=True)
    returned = returned.reshape(all_experts, capacity, model_width)
    picked_rows = returned[flat_picks, slot_index].reshape(token_count, top_count, model_width)
    mixed_rows = jnp.einsum(
        "tk,tkd->td", gate_prob[0], picked_rows, preferred_element_type=jnp.float32
    )
    return mixed_rows.astype(jnp.bfloat16)[None]


def solution(mesh):
    return jax.shard_map(
        per_device,
        mesh=mesh,
        in_specs=(
            P("rep", "tok", None),
            P("rep", "tok", None),
            P("rep", "tok", None),
            P("tok", "rep", None),
            P("tok", "rep", None),
        ),
        out_specs=P("rep", "tok", None),
        check_vma=False,
    )
```

profile of v0, /device:TPU:14, one launch (start us, length us, event | category | flops | bytes accessed | tf_op | source)
XLA Modules:
  0.0 991.7 jit_solution(9819914999492072566)
XLA Ops:
  6.5 9.0 convert_element_type.27
  15.7 6.1 convert_element_type.29
  21.8 0.1 copy.13
  21.9 0.1 eq.29
  22.0 0.1 eq.25
  22.1 0.1 reshape_squeeze.3
  22.2 9.0 reduce-window.6
  31.2 0.1 slice.20
  31.3 0.1 copy.16
  31.5 0.1 broadcast_add_fusion
  31.7 0.1 multiply_reduce_fusion
  31.8 0.1 and_reduce_fusion
  31.9 4.3 scatter_custom_fusion
  36.3 0.1 reshape.74
  36.4 0.1 reshape.77
  36.6 6.0 gather_fusion
  42.5 7.3 reshape.68
  49.9 6.2 copy.18
  56.1 56.4 %all_to_all.10 = bf16[8,4,36,2048]{3,1,2,0:T(4,128)(2,1)} all-to-all(bf16[8,4,36,2048]{3,1,2,0:T(4,128)(2,1)S(1)} %copy.18), channel_id=1, replica_groups=mesh['tok'=8,'rep'=4] {'tok'}, dimensions={0} | all-to-all | bytes 9437184 | tf_op jit(solution)/shard_map/all_to_all | solution.py:41
  112.5 463.0 %all-gather.3.cloned.1.call-done = bf16[4,2048,2048]{2,1,0:T(8,128)(2,1)} async-done(((bf16[4,512,2048]{2,1,0:T(8,128)(2,1)}), bf16[4,2048,2048]{2,1,0:T(8,128)(2,1)}) %all-gather.3.cloned.1.call-update) | async-done | bytes 33554448 | tf_op jit(solution)/shard_map/all_gather | solution.py:21
  575.5 31.2 %fusion.6 = f32[8,4,36,2048]{3,2,0,1:T(8,128)} fusion(bf16[4,2048,2048]{2,1,0:T(8,128)(2,1)} %all-gather.3.cloned.1.call-done, bf16[8,4,36,2048]{3,1,2,0:T(4,128)(2,1)} %all_to_all.10), kind=kOutput, calls=%fused_computation.11 | convolution fusion | flops 9663676416 | bytes 47710208 | tf_op jit(solution)/shard_map/secd,edf->secf/dot_general | solution.py:42
  606.7 255.4 %all-gather.5.cloned.1.call-done = bf16[4,1024,2048]{2,1,0:T(8,128)(2,1)} async-done(((bf16[4,256,2048]{2,1,0:T(8,128)(2,1)}), bf16[4,1024,2048]{2,1,0:T(8,128)(2,1)}) %all-gather.5.cloned.1.call-update) | async-done | bytes 16777232 | tf_op jit(solution)/shard_map/all_gather | solution.py:22
  862.1 13.9 %convert_bitcast_fusion = bf16[8,4,36,2048]{3,2,0,1:T(8,128)(2,1)S(1)} fusion(bf16[4,1024,2048]{2,1,0:T(8,128)(2,1)} %all-gather.5.cloned.1.call-done, f32[8,4,36,2048]{3,2,0,1:T(8,128)} %fusion.6), kind=kOutput, calls=%fused_computation.10 | convolution fusion | flops 4841275392 | bytes 30932992 | tf_op jit(solution)/shard_map/secf,efd->secd/dot_general | solution.py:46
  876.0 5.9 copy.20
  881.9 4.9 all-to-all-start.1
  886.8 0.1 copy.24
  887.0 52.4 %all-to-all-done.1 = bf16[8,4,36,2048]{3,1,2,0:T(4,128)(2,1)} async-done(((bf16[8,4,36,2048]{3,1,2,0:T(4,128)(2,1)}), bf16[8,4,36,2048]{3,1,2,0:T(4,128)(2,1)}, u32[]{:S(2)}, u32[]{:S(2)}) %all-to-all-start.1) | async-done | bytes 4718624 | tf_op jit(solution)/shard_map/all_to_all | solution.py:50
  939.3 7.9 copy.21
  947.2 7.7 reshape.69
  954.9 25.4 %gather_fusion.1 = bf16[1024,2048]{1,0:T(8,128)(2,1)} fusion(bf16[32,36,2048]{2,0,1:T(8,128)(2,1)} %reshape.69, s32[1024]{0:T(1024)S(1)} %bitcast.55), kind=kCustom, calls=%fused_computation.1 | custom fusion | bytes 8396800 | tf_op jit(solution)/shard_map/gather | solution.py:52
  980.3 3.4 fusion.11
  983.8 1.1 copy.35
  (24 shorter events, 0.3 us)
Async XLA Ops:
  6.5 569.0 %all-gather.3.cloned.1.call-start = ((), (), s32[]{:S(2)}) async-start(), calls=%async_computation.2 | async-start | bytes 41943040 | tf_op jit(solution)/shard_map/all_gather | solution.py:21
  15.6 6.2 copy-start.1
  15.6 846.5 %all-gather.5.cloned.1.call-start = ((), (), s32[]{:S(2)}) async-start(), calls=%async_computation.3 | async-start | bytes 20971520 | tf_op jit(solution)/shard_map/all_gather | solution.py:22
  21.7 10.0 %copy-start.4 = (s32[2]{0:T(128)S(1)}, s32[2]{0:T(128)}, u32[]{:S(2)}) copy-start(s32[2]{0:T(128)} %constant.45) | copy-start | bytes 28
  21.7 10.1 %copy-start.3 = (s32[2]{0:T(128)S(1)}, s32[2]{0:T(128)}, u32[]{:S(2)}) copy-start(s32[2]{0:T(128)} %constant.48) | copy-start | bytes 28
  21.7 14.7 %copy-start = (bf16[1,128,2048]{2,1,0:T(8,128)(2,1)S(1)}, bf16[1,128,2048]{2,1,0:T(8,128)(2,1)}, u32[]{:S(2)}) copy-start(bf16[1,128,2048]{2,1,0:T(8,128)(2,1)} %param.5) | copy-start | bytes 1572868
  881.9 4.9 copy-start.2
  881.9 57.4 %all-to-all-start.1 = ((bf16[8,4,36,2048]{3,1,2,0:T(4,128)(2,1)}), bf16[8,4,36,2048]{3,1,2,0:T(4,128)(2,1)}, u32[]{:S(2)}, u32[]{:S(2)}) async-start(bf16[8,4,36,2048]{3,1,2,0:T(4,128)(2,1)} %copy.20), calls=%async_computation.1 | async-start | bytes 9437184 | tf_op jit(solution)/shard_map/all_to_all | solution.py:50
Sparse Core Ops, SparseCore 0:
  15.7 559.7 all-gather.2
  577.1 284.9 all-gather.4
where the time goes:
time: 999 us; the launch traced here: 992 us
  waiting for transfers between devices  771 us (77%)
  local copies, waits for them, and re-layouts  72.9 us (7%)
  blocking collectives  56.4 us (6%)
  matrix products  48.5 us (5%)
  other arithmetic  24.5 us (2%)
  between operations  13.6 us (1%)
    all_gather x1, waiting for transfers between devices, per_device(): lax.all_gather(served_gate, 'rep', axis=1, tiled=True)  463 us
    all_gather x1, waiting for transfers between devices, per_device(): lax.all_gather(served_down, 'rep', axis=1, tiled=True)  255 us
    all_to_all x1, blocking collectives, per_device(): lax.all_to_all(send_rows, 'tok', split_axis=0, concat_axis=0, tiled=True)  56.4 us
    all_to_all x1, waiting for transfers between devices, per_device(): lax.all_to_all(expert_out, 'tok', split_axis=0, concat_axis=0, tiled=True)  52.4 us
    dot_general x1, matrix products, per_device(): jnp.einsum('secd,edf->secf', arrived, full_gate, preferred_element_type=j...  31.2 us
    gather x1, local copies, waits for them, and re-layouts, per_device(): returned[flat_picks, slot_index]  25.4 us
  transfers between devices with their start and end apart: 3, of which 3 were waited for; matrix products, arithmetic and copies ran while one was open for 7% of the time, Pallas kernels for 0%

commit v1 on v0

v1 whole, which is shorter than its diff:
```python
import jax
import jax.numpy as jnp
from jax import lax
from jax.sharding import PartitionSpec as P

GATHER_BYTES = 16 << 20


def reshard_gate_up(gate_up, reps):
    experts, rows, columns = gate_up.shape
    part = columns // 2 // reps
    me = lax.axis_index("rep")
    pieces = (
        gate_up.astype(jnp.bfloat16)
        .reshape(experts, rows, 2, reps, part)
        .transpose(3, 2, 1, 0, 4)
        .reshape(reps, 2, rows, experts * part)
    )
    whole = jnp.zeros((2, reps, rows, experts * part), jnp.bfloat16)
    for shift in range(reps):
        piece = lax.dynamic_index_in_dim(pieces, lax.rem(me + shift, reps), 0, keepdims=False)
        if shift:
            piece = lax.ppermute(piece, "rep", [(i, (i + shift) % reps) for i in range(reps)])
        source = lax.rem(me + reps - shift, reps)
        whole = lax.dynamic_update_slice(whole, piece[:, None], (0, source, 0, 0))
    whole = whole.reshape(2, reps * rows, experts * part)
    return whole[0], whole[1]


def per_device(hidden_states, routes, gate_prob, gate_up, down):
    groups = lax.axis_size("tok")
    reps = lax.axis_size("rep")
    experts = gate_up.shape[0]
    _, token_count, width = hidden_states.shape
    part = gate_up.shape[2] // 2 // reps
    all_experts = groups * experts
    tokens = hidden_states[0]
    total_bytes = groups * reps * token_count * width * 2
    chunks = max(1, total_bytes // GATHER_BYTES)
    chunk = token_count // chunks

    hit = routes[0][:, :, None] == jnp.arange(all_experts, dtype=jnp.int32)
    weight = jnp.sum(jnp.where(hit, gate_prob[0][:, :, None], 0.0), axis=1)
    gate, up = reshard_gate_up(gate_up, reps)
    stacked_down = down.astype(jnp.bfloat16).reshape(experts * part, width)
    first = lax.axis_index("tok") * experts

    def one_chunk(rows, row_weight):
        everyone = lax.all_gather(rows, ("rep", "tok"), axis=0, tiled=True)
        all_weight = lax.all_gather(row_weight, ("rep", "tok"), axis=0, tiled=True)
        mine = lax.dynamic_slice_in_dim(all_weight, first, experts, 1)
        scale = jnp.repeat(mine, part, axis=1)
        g = jnp.dot(everyone, gate, preferred_element_type=jnp.float32)
        u = jnp.dot(everyone, up, preferred_element_type=jnp.float32)
        units = (jax.nn.silu(g) * u * scale).astype(jnp.bfloat16)
        partial = jnp.dot(units, stacked_down, preferred_element_type=jnp.float32)
        return lax.psum_scatter(
            partial.astype(jnp.bfloat16), ("rep", "tok"), scatter_dimension=0, tiled=True
        )

    if chunks == 1:
        return one_chunk(tokens, weight)[None]
    mixed = lax.map(
        lambda part_of: one_chunk(*part_of),
        (tokens.reshape(chunks, chunk, width), weight.reshape(chunks, chunk, all_experts)),
    )
    return mixed.reshape(1, token_count, width)


def solution(mesh):
    return jax.shard_map(
        per_device,
        mesh=mesh,
        in_specs=(
            P("rep", "tok", None),
            P("rep", "tok", None),
            P("rep", "tok", None),
            P("tok", "rep", None),
            P("tok", "rep", None),
        ),
        out_specs=P("rep", "tok", None),
        check_vma=False,
    )
```

time: 999 us -> 591 us (0.59)
  waiting for transfers between devices: 771 us -> 186 us
  blocking collectives: 56.4 us -> 254 us
  matrix products: 48.5 us -> 73.4 us
  local copies, waits for them, and re-layouts: 72.9 us -> 52.8 us
  other arithmetic: 24.5 us -> 6.14 us
    all_gather x2 -> x1, waiting for transfers between devices: 718 us -> 0.01 us  [one_chunk(): everyone = lax.all_gather(rows, ('rep', 'tok'), axis=0, tiled=True)]
    all_gather x0 -> x1, blocking collectives: none -> 254 us  [one_chunk(): all_weight = lax.all_gather(row_weight, ('rep', 'tok'), axis=0, tiled=True)]
    reduce_scatter x0 -> x1, waiting for transfers between devices: none -> 185 us  [one_chunk(): lax.psum_scatter(partial.astype(jnp.bfloat16), ('rep', 'tok'), scatter_di...]
    all_to_all x1 -> x0, blocking collectives: 56.4 us -> none  [per_device(): lax.all_to_all(send_rows, 'tok', split_axis=0, concat_axis=0, tiled=True)]
    all_to_all x1 -> x0, waiting for transfers between devices: 52.4 us -> none  [per_device(): lax.all_to_all(expert_out, 'tok', split_axis=0, concat_axis=0, tiled=True)]
    gather x2 -> x0, local copies, waits for them, and re-layouts: 31.4 us -> none  [the longest x1 25.4 us: per_device(): returned[flat_picks, slot_index]]
    dot_general x3, matrix products: 48.5 us -> 73.4 us  [the longest x1 25.8 us: one_chunk(): u = jnp.dot(everyone, up, preferred_element_type=jnp.float32)]
    reshape x3 -> x0, local copies, waits for them, and re-layouts: 21.2 us -> none  [the longest x2 13.5 us: per_device(): padded_rows[slot_table]]
  transfers between devices with their start and end apart: 3 -> 5, of which waited for: 3 -> 1; matrix products, arithmetic and copies ran while one was open for 7% -> 10% of each run, Pallas kernels for 0% -> 0%
where the time goes in v1:
time: 591 us; the launch traced here: 590 us
  blocking collectives  254 us (43%)
  waiting for transfers between devices  186 us (31%)
  matrix products  73.4 us (12%)
  local copies, waits for them, and re-layouts  52.8 us (9%)
  between operations  13.5 us (2%)
  other arithmetic  6.14 us (1%)
    all_gather x1, blocking collectives, one_chunk(): all_weight = lax.all_gather(row_weight, ('rep', 'tok'), axis=0, tiled=True)  254 us
    reduce_scatter x1, waiting for transfers between devices, one_chunk(): lax.psum_scatter(partial.astype(jnp.bfloat16), ('rep', 'tok'), scatter_di...  185 us
    dot_general x1, matrix products, one_chunk(): u = jnp.dot(everyone, up, preferred_element_type=jnp.float32)  25.8 us
    dot_general x1, matrix products, one_chunk(): g = jnp.dot(everyone, gate, preferred_element_type=jnp.float32)  23.8 us
    dot_general x1, matrix products, one_chunk(): partial = jnp.dot(units, stacked_down, preferred_element_type=jnp.float32)  23.7 us
    dynamic_slice x4, local copies, waits for them, and re-layouts, reshard_gate_up(): lax.dynamic_index_in_dim(pieces, lax.rem(me + shift, reps), 0, keepdims=F...  18.5 us
    unnamed x11, local copies, waits for them, and re-layouts  13.7 us
  transfers between devices with their start and end apart: 5, of which 1 were waited for; matrix products, arithmetic and copies ran while one was open for 10% of the time, Pallas kernels for 0%

profile of v1, /device:TPU:14, one launch (start us, length us, event | category | flops | bytes accessed | tf_op | source)
XLA Modules:
  0.0 589.9 jit_solution(145223139288370264)
XLA Ops:
  6.5 0.0 all-gather.3.cloned.1.call-start
  6.5 0.7 all-gather.3.cloned.1.call-update
  7.3 0.0 reduce-scatter.2.cloned.1.call-start
  7.3 13.7 %copy.26 = bf16[4,512,2048]{1,2,0:T(8,128)(2,1)} copy(f32[4,512,2048]{2,1,0:T(8,128)} %param.8) | data formatting | bytes 25165824 | tf_op args[3]
  21.0 7.5 %copy.27 = bf16[4,2,512,4,256]{2,4,3,1,0:T(8,128)(2,1)} copy(bf16[4,2,512,4,256]{2,4,0,1,3:T(8,128)(2,1)} %bitcast.59) | data formatting | bytes 16777216 | tf_op jit(solution)/shard_map/transpose | solution.py:16
  28.5 6.3 %constant_dynamic-slice_fusion.1 = (bf16[1,2,512,1024]{2,3,1,0:T(8,128)(2,1)}, bf16[1,2,512,1024]{2,3,1,0:T(8,128)(2,1)}, bf16[1,2,512,1024]{2,3,1,0:T(8,128)(2,1)}, bf16[2,1,512,1024]{2,3,0,1:T(8,128)(2,1)S(1)}) fusion(bf16[4,2,512,1024]{2,3,1,0:T(8,128)(2,1)} %bitcast.60, s32[]{:T(128)S(6)} %select_n.29, s32[]{:T(128)S(6)} %select_n.30, s32[]{:T(128)S(6)} %select_n.28, ...), kind=kLoop, calls=%fused_computation.20 | loop fusion | bytes 16777232 | tf_op jit(solution)/shard_map/jit(dynamic_index_in_dim)/dynamic_slice | solution.py:21
  34.9 4.0 copy.30
  38.9 1.5 collective-permute-start
  40.4 4.2 copy.32
  44.6 1.1 collective-permute-start.1
  45.7 4.0 copy.34
  49.7 1.9 collective-permute-start.2
  51.6 2.5 copy.29
  54.1 6.1 %convert_element_type.14 = bf16[4,256,2048]{2,1,0:T(8,128)(2,1)} convert(f32[4,256,2048]{2,1,0:T(8,128)} %param.9) | non-fusion elementwise | flops 2097152 | bytes 12582912 | tf_op jit(solution)/shard_map/convert_element_type | solution.py:45
  60.2 0.0 copy-done.3
  60.2 0.0 copy-done.4
  60.2 1.1 broadcast_in_dim.36
  61.3 0.0 copy-done
  61.3 0.3 constant_dynamic-update-slice_fusion
  61.6 253.6 %all_gather.7 = f32[4096,32]{0,1:T(8,128)S(1)} all-gather(f32[128,32]{0,1:T(8,128)S(1)} %select_reduce_fusion), channel_id=1, replica_groups=mesh['tok'=8,'rep'=4] {'rep','tok'}, dimensions={0}, use_global_device_ids=true | all-gather | bytes 540672 | tf_op jit(solution)/shard_map/all_gather | solution.py:50
  315.3 0.0 collective-permute-done
  315.3 1.9 bitcast_dynamic-update-slice_fusion.2
  317.1 0.0 collective-permute-done.1
  317.2 1.9 bitcast_dynamic-update-slice_fusion.1
  319.0 0.0 collective-permute-done.2
  319.0 1.9 bitcast_dynamic-update-slice_fusion
  320.9 3.7 fusion.10
  324.6 23.8 %fusion.6 = f32[1024,4096]{1,0:T(8,128)} fusion(bf16[2048,1024]{1,0:T(8,128)(2,1)} %bitcast.63, bf16[1,4096,2048]{2,1,0:T(8,128)(2,1)} %all-gather.3.cloned.1.call-done), kind=kOutput, calls=%fused_computation.10 | convolution fusion | flops 17179869184 | bytes 37748736 | tf_op jit(solution)/shard_map/dot_general | solution.py:53
  348.4 25.8 %fusion = bf16[4096,1024]{0,1:T(8,128)(2,1)} fusion(f32[1024,4096]{1,0:T(8,128)} %fusion.6, f32[4096,4]{0,1:T(4,128)S(1)} %constant_dynamic-slice_fusion, bf16[2048,1024]{1,0:T(8,128)(2,1)S(1)} %bitcast.62, bf16[1,4096,2048]{2,1,0:T(8,128)(2,1)} %all-gather.3.cloned.1.call-done), kind=kOutput, calls=%fused_computation.1 | convolution fusion | flops 17209229312 | bytes 46202880 | tf_op jit(solution)/shard_map/dot_general | solution.py:54
  374.2 23.7 %convolution_convert_fusion = bf16[4096,2048]{1,0:T(8,128)(2,1)} fusion(bf16[4096,1024]{0,1:T(8,128)(2,1)} %fusion, bf16[1024,2048]{1,0:T(8,128)(2,1)S(1)} %bitcast.61), kind=kOutput, calls=%fused_computation.12 | convolution fusion | flops 17188257792 | bytes 29360128 | tf_op jit(solution)/shard_map/dot_general | solution.py:56
  398.0 0.0 reduce-scatter.2.cloned.1.call-update
  398.0 185.1 %reduce-scatter.2.cloned.1.call-done = bf16[128,2048]{1,0:T(8,128)(2,1)} async-done(((bf16[4096,2048]{1,0:T(8,128)(2,1)}), bf16[128,2048]{1,0:T(8,128)(2,1)}) %reduce-scatter.2.cloned.1.call-update) | async-done | bytes 524304 | tf_op jit(solution)/shard_map/reduce_scatter | solution.py:57
  (10 shorter events, 0.0 us)
Async XLA Ops:
  6.5 318.1 %all-gather.3.cloned.1.call-start = ((), (), s32[]{:S(2)}) async-start(), calls=%async_computation.2 | async-start | bytes 17301504 | tf_op jit(solution)/shard_map/all_gather | solution.py:49
  7.3 575.8 %reduce-scatter.2.cloned.1.call-start = ((), (), s32[]{:S(2)}) async-start(), calls=%async_computation.1 | async-start | bytes 17301504 | tf_op jit(solution)/shard_map/reduce_scatter | solution.py:57
  38.9 276.4 %collective-permute-start = (bf16[2,512,1024]{2,1,0:T(8,128)(2,1)}, bf16[2,512,1024]{2,1,0:T(8,128)(2,1)}, u32[]{:S(2)}, u32[]{:S(2)}) collective-permute-start(bf16[2,512,1024]{2,1,0:T(8,128)(2,1)} %bitcast.66), channel_id=1, source_target_pairs={{0,1},{1,2},{2,3},{3,0},{4,5},{5,6},{6,7},{7,4},{8,9},{9,10},{10,1... | collective-permute-start | bytes 6291464 | tf_op jit(solution)/shard_map/ppermute | solution.py:23
  44.6 272.5 %collective-permute-start.1 = (bf16[2,512,1024]{2,1,0:T(8,128)(2,1)}, bf16[2,512,1024]{2,1,0:T(8,128)(2,1)}, u32[]{:S(2)}, u32[]{:S(2)}) collective-permute-start(bf16[2,512,1024]{2,1,0:T(8,128)(2,1)} %bitcast.65), channel_id=1, source_target_pairs={{0,2},{1,3},{2,0},{3,1},{4,6},{5,7},{6,4},{7,5},{8,10},{9,11},{10,... | collective-permute-start | bytes 6291464 | tf_op jit(solution)/shard_map/ppermute | solution.py:23
  49.7 269.4 %collective-permute-start.2 = (bf16[2,512,1024]{2,1,0:T(8,128)(2,1)}, bf16[2,512,1024]{2,1,0:T(8,128)(2,1)}, u32[]{:S(2)}, u32[]{:S(2)}) collective-permute-start(bf16[2,512,1024]{2,1,0:T(8,128)(2,1)} %bitcast.64), channel_id=1, source_target_pairs={{0,3},{1,0},{2,1},{3,2},{4,7},{5,4},{6,5},{7,6},{8,11},{9,8},{10,9... | collective-permute-start | bytes 6291464 | tf_op jit(solution)/shard_map/ppermute | solution.py:23
  51.6 8.6 %copy-start.3 = (f32[1,128,8]{1,2,0:T(8,128)S(1)}, f32[1,128,8]{1,2,0:T(8,128)}, u32[]{:S(2)}) copy-start(f32[1,128,8]{1,2,0:T(8,128)} %param.7) | copy-start | bytes 12292
  51.6 8.6 %copy-start.4 = (s32[1,128,8]{1,2,0:T(8,128)S(1)}, s32[1,128,8]{1,2,0:T(8,128)}, u32[]{:S(2)}) copy-start(s32[1,128,8]{1,2,0:T(8,128)} %param.6) | copy-start | bytes 12292
  54.1 7.2 %copy-start = (bf16[2,1,512,1024]{3,2,1,0:T(8,128)(2,1)S(1)}, bf16[2,1,512,1024]{3,2,1,0:T(8,128)(2,1)}, u32[]{:S(2)}) copy-start(bf16[2,1,512,1024]{3,2,1,0:T(8,128)(2,1)} %copy.29) | copy-start | bytes 6291460
  324.6 23.8 %copy-start.2 = (bf16[1,4,512,1024]{3,2,1,0:T(8,128)(2,1)S(1)}, bf16[1,4,512,1024]{3,2,1,0:T(8,128)(2,1)}, u32[]{:S(2)}) copy-start(bf16[1,4,512,1024]{3,2,1,0:T(8,128)(2,1)} %get-tuple-element.5) | copy-start | bytes 12582916
  348.4 25.8 %copy-start.1 = (bf16[4,256,2048]{2,1,0:T(8,128)(2,1)S(1)}, bf16[4,256,2048]{2,1,0:T(8,128)(2,1)}, u32[]{:S(2)}) copy-start(bf16[4,256,2048]{2,1,0:T(8,128)(2,1)} %convert_element_type.14) | copy-start | bytes 12582916
Sparse Core Ops, SparseCore 0:
  10.2 255.6 all-gather.2
  398.1 184.9 reduce-scatter.1

commit v2 on v1

--- a/solution.py
+++ b/solution.py
@@ -1,6 +1,8 @@
 import jax
 import jax.numpy as jnp
 from jax import lax
+from jax.experimental import pallas as pl
+from jax.experimental.pallas import tpu as pltpu
 from jax.sharding import PartitionSpec as P
 
 GATHER_BYTES = 16 << 20
@@ -27,6 +29,278 @@
     return whole[0], whole[1]
 
 
+LANES = 128
+HALVES = 2
+
+
+def fused_kernel(
+    x_ref, sel_ref, gate_ref, down_ref, out_ref,
+    x, w, d, units, r1, r2, r3, rz,
+    local_sem, w_send, w_recv, z_send, z_recv, ag_send, ag_recv, rs_send, rs_recv, o_send, o_recv,
+):
+    reps, _, _, _, rows, _ = x.shape
+    experts, depth, both = w.shape
+    part = both // 2
+    width = d.shape[1]
+    block_depth = depth // reps
+    ff = gate_ref.shape[2] // 2
+    r = lax.axis_index("rep")
+    t = lax.axis_index("tok")
+    core = lax.rem(t, 2)
+    xs = lax.rem(lax.div(t, 2), 2)
+    ys = lax.div(t, 4)
+    core_mate = {"tok": t + 1 - 2 * core}
+    x_mate = {"tok": t + 2 - 4 * xs}
+    y_mate = {"tok": t + 4 - 8 * ys}
+    rep_mates = [{"rep": lax.rem(r + k, reps)} for k in range(1, reps)]
+    other = 1 - core
+
+    barrier = pltpu.get_barrier_semaphore()
+    mates = [core_mate, x_mate, y_mate] + rep_mates
+    for mate in mates:
+        pl.semaphore_signal(barrier, inc=1, device_id=mate, device_id_type=pl.DeviceIdType.MESH)
+    pl.semaphore_wait(barrier, len(mates))
+
+    def remote(src, dst, send, recv, mate):
+        copy = pltpu.make_async_remote_copy(
+            src_ref=src, dst_ref=dst, send_sem=send, recv_sem=recv,
+            device_id=mate, device_id_type=pl.DeviceIdType.MESH,
+        )
+        copy.start()
+        return copy
+
+    def local(src, dst, sem):
+        copy = pltpu.make_async_copy(src, dst, sem)
+        copy.start()
+        return copy
+
+    own_x = local(x_ref, x.at[r, ys, xs, core], local_sem.at[0])
+    to_reps = [
+        remote(x_ref, x.at[r, ys, xs, core], z_send.at[k], z_recv.at[k], rep_mates[k])
+        for k in range(reps - 1)
+    ]
+    landing = pl.ds(pl.multiple_of(r * block_depth, block_depth), block_depth)
+
+    def send_weights(e):
+        copies = []
+        for half in range(HALVES):
+            into = w.at[e, landing, pl.ds(half * part, part)]
+            for k in range(1, reps):
+                to = lax.rem(r + k, reps)
+                columns = pl.ds(pl.multiple_of(half * ff + to * part, part), part)
+                copies.append(
+                    remote(
+                        gate_ref.at[e, :, columns], into,
+                        w_send.at[e, k - 1, half], w_recv.at[e, k - 1, half], rep_mates[k - 1],
+                    )
+                )
+            columns = pl.ds(pl.multiple_of(half * ff + r * part, part), part)
+            copies.append(
+                local(gate_ref.at[e, :, columns], into, local_sem.at[2 + HALVES * e + half])
+            )
+        return copies
+
+    weights = [send_weights(e) for e in range(experts - 1)]
+    own_d = local(down_ref, d, local_sem.at[1])
+
+    own_x.wait()
+    chunk_of = [lax.rem(r + reps - i, reps) for i in range(reps)]
+    stage = []
+    for i in range(reps):
+        if i:
+            to_reps[i - 1].wait()
+        mine = x.at[chunk_of[i], ys, xs, core]
+        mate = x_mate if i % 2 == 0 else y_mate
+        stage.append(remote(mine, mine, ag_send.at[i, 0], ag_recv.at[i, 0], mate))
+    for i in range(reps):
+        stage[i].wait()
+        if i % 2 == 0:
+            mine, mate = x.at[chunk_of[i], ys, :, core], y_mate
+        else:
+            mine, mate = x.at[chunk_of[i], :, xs, core], x_mate
+        stage[i] = remote(mine, mine, ag_send.at[i, 1], ag_recv.at[i, 1], mate)
+    for i in range(reps):
+        stage[i].wait()
+        mine = x.at[chunk_of[i], :, :, core]
+        stage[i] = remote(mine, mine, ag_send.at[i, 2], ag_recv.at[i, 2], core_mate)
+    weights.append(send_weights(experts - 1))
+    for i in range(reps):
+        stage[i].wait()
+
+    def make_units(e, i, half):
+        c = lax.rem(r + 1 + i, reps)
+        h = other + half * (core - other)
+        values = x[c, :, :, h, :, pl.ds(0, width)].reshape(4 * rows, width)
+        marks = x[c, :, :, h, :, pl.ds(width, LANES)].reshape(4 * rows, LANES)
+        y = jnp.dot(values, w[e], preferred_element_type=jnp.float32)
+        scale = jnp.dot(marks, sel_ref[e], preferred_element_type=jnp.float32)
+        g, u = y[:, :part], y[:, part:]
+        unit = g * (1.0 / (1.0 + jnp.exp(-g))) * u * scale
+        units[i, half, :, pl.ds(e * part, part)] = unit.astype(jnp.bfloat16)
+
+    def project(i, half):
+        c = lax.rem(r + 1 + i, reps)
+        h = other if half == 0 else core
+        step = 512
+
+        def columns_of(n, carry):
+            columns = pl.ds(pl.multiple_of(n * step, step), step)
+            total = jnp.dot(units[i, half], d[:, columns], preferred_element_type=jnp.float32)
+            total = total.reshape(2, 2, rows, step)
+            if half:
+                total = total + r1[i, :, :, :, columns].astype(jnp.float32)
+            x[c, :, :, h, :, columns] = total.astype(jnp.bfloat16)
+            return carry
+
+        lax.fori_loop(0, width // step, columns_of, 0)
+
+    for e in range(experts - 1):
+        for copy in weights[e]:
+            copy.wait()
+
+        def tile(n, carry):
+            make_units(e, lax.div(n, 2), lax.rem(n, 2))
+            return carry
+
+        lax.fori_loop(0, 2 * reps, tile, 0)
+    for copy in weights[experts - 1]:
+        copy.wait()
+    own_d.wait()
+
+    flat = pl.ds(0, width)
+    first, second, third, last = {}, {}, {}, []
+
+    def scatter_core(i):
+        make_units(experts - 1, i, 0)
+        project(i, 0)
+        c = lax.rem(r + 1 + i, reps)
+        first[i] = remote(
+            x.at[c, :, :, other, :, flat], r1.at[i], rs_send.at[i, 0], rs_recv.at[i, 0], core_mate
+        )
+
+    def scatter_second(i):
+        make_units(experts - 1, i, 1)
+        first[i].wait_recv()
+        project(i, 1)
+        c = lax.rem(r + 1 + i, reps)
+        if i % 2 == 0:
+            src, mate = x.at[c, :, 1 - xs, core, :, flat], x_mate
+        else:
+            src, mate = x.at[c, 1 - ys, :, core, :, flat], y_mate
+        second[i] = remote(src, r2.at[i], rs_send.at[i, 1], rs_recv.at[i, 1], mate)
+
+    def scatter_third(i):
+        second[i].wait_recv()
+        c = lax.rem(r + 1 + i, reps)
+
+        def add(n, carry):
+            at = pl.ds(pl.multiple_of(n * 16, 16), 16)
+            for k in range(2):
+                where = (c, k, xs, core, at, flat) if i % 2 == 0 else (c, ys, k, core, at, flat)
+                total = x[where].astype(jnp.float32) + r2[i, k, at, :].astype(jnp.float32)
+                x[where] = total.astype(jnp.bfloat16)
+            return carry
+
+        lax.fori_loop(0, rows // 16, add, 0)
+        if i % 2 == 0:
+            src, mate = x.at[c, 1 - ys, xs, core, :, flat], y_mate
+        else:
+            src, mate = x.at[c, ys, 1 - xs, core, :, flat], x_mate
+        third[i] = remote(src, r3.at[i], rs_send.at[i, 2], rs_recv.at[i, 2], mate)
+
+    def scatter_rep(i):
+        third[i].wait_recv()
+        c = lax.rem(r + 1 + i, reps)
+        if i == reps - 1:
+            return
+
+        def add(n, carry):
+            at = pl.ds(pl.multiple_of(n * 16, 16), 16)
+            where = (c, ys, xs, core, at, flat)
+            total = x[where].astype(jnp.float32) + r3[i, at, :].astype(jnp.float32)
+            x[where] = total.astype(jnp.bfloat16)
+            return carry
+
+        lax.fori_loop(0, rows // 16, add, 0)
+        last.append(
+            remote(
+                x.at[c, ys, xs, core, :, flat], rz.at[i], o_send.at[i], o_recv.at[i], rep_mates[i]
+            )
+        )
+
+    for step in range(reps + 3):
+        if step < reps:
+            scatter_core(step)
+        for lag, work in ((1, scatter_second), (2, scatter_third), (3, scatter_rep)):
+            if 0 <= step - lag < reps:
+                work(step - lag)
+    for copy in last:
+        copy.wait_recv()
+
+    def finish(n, carry):
+        at = pl.ds(pl.multiple_of(n * 16, 16), 16)
+        total = x[r, ys, xs, core, at, flat].astype(jnp.float32)
+        total = total + r3[reps - 1, at, :].astype(jnp.float32)
+        for k in range(reps - 1):
+            total = total + rz[k, at, :].astype(jnp.float32)
+        out_ref[at, :] = total.astype(jnp.bfloat16)
+        return carry
+
+    lax.fori_loop(0, rows // 16, finish, 0)
+    for copy in list(first.values()) + list(second.values()) + list(third.values()) + last:
+        copy.wait_send()
+
+
+def fused(tokens, weight, gate_up, down, reps):
+    rows, width = tokens.shape
+    experts, block_depth, columns = gate_up.shape
+    part = columns // 2 // reps
+    all_experts = weight.shape[1]
+    high = lax.reduce_precision(weight, 8, 7)
+    marks = jnp.concatenate([high, weight - high], axis=1).astype(jnp.bfloat16)
+    marks = jnp.pad(marks, ((0, 0), (0, LANES - 2 * all_experts)))
+    x = jnp.concatenate([tokens, marks], axis=1)
+    lane = jnp.arange(LANES, dtype=jnp.int32)
+    own = lax.axis_index("tok") * experts + jnp.arange(experts, dtype=jnp.int32)
+    chosen = (lane[None, :] == own[:, None]) | (lane[None, :] == own[:, None] + all_experts)
+    sel = jnp.broadcast_to(chosen[:, :, None], (experts, LANES, part)).astype(jnp.bfloat16)
+    depth = block_depth * reps
+    bf16 = jnp.bfloat16
+    dma = pltpu.SemaphoreType.DMA
+    hbm = pl.BlockSpec(memory_space=pl.ANY)
+    vmem = pl.BlockSpec(memory_space=pltpu.VMEM)
+    return pl.pallas_call(
+        fused_kernel,
+        out_shape=jax.ShapeDtypeStruct((rows, width), bf16),
+        in_specs=[hbm, vmem, hbm, hbm],
+        out_specs=vmem,
+        scratch_shapes=[
+            pltpu.VMEM((reps, 2, 2, 2, rows, width + LANES), bf16),
+            pltpu.VMEM((experts, depth, 2 * part), bf16),
+            pltpu.VMEM((experts * part, width), bf16),
+            pltpu.VMEM((reps, 2, 4 * rows, experts * part), bf16),
+            pltpu.VMEM((reps, 2, 2, rows, width), bf16),
+            pltpu.VMEM((reps, 2, rows, width), bf16),
+            pltpu.VMEM((reps, rows, width), bf16),
+            pltpu.VMEM((reps - 1, rows, width), bf16),
+            dma((2 + HALVES * experts,)),
+            dma((experts, reps - 1, HALVES)),
+            dma((experts, reps - 1, HALVES)),
+            dma((reps - 1,)),
+            dma((reps - 1,)),
+            dma((reps, 3)),
+            dma((reps, 3)),
+            dma((reps, 3)),
+            dma((reps, 3)),
+            dma((reps - 1,)),
+            dma((reps - 1,)),
+        ],
+        compiler_params=pltpu.CompilerParams(
+            collective_id=0, has_side_effects=True, vmem_limit_bytes=62 << 20
+        ),
+    )(x, sel, gate_up.astype(bf16), down.astype(bf16).reshape(experts * part, width))
+
+
 def per_device(hidden_states, routes, gate_prob, gate_up, down):
     groups = lax.axis_size("tok")
     reps = lax.axis_size("rep")
@@ -41,6 +315,8 @@
 
     hit = routes[0][:, :, None] == jnp.arange(all_experts, dtype=jnp.int32)
     weight = jnp.sum(jnp.where(hit, gate_prob[0][:, :, None], 0.0), axis=1)
+    if chunks == 1 and groups == 8 and reps == 4 and 2 * all_experts <= LANES:
+        return fused(tokens, weight, gate_up, down, reps)[None]
     gate, up = reshard_gate_up(gate_up, reps)
     stacked_down = down.astype(jnp.bfloat16).reshape(experts * part, width)
     first = lax.axis_index("tok") * experts

time: 591 us -> 370 us (0.63)
  Pallas kernels: 0 us -> 347 us
  blocking collectives: 254 us -> 0 us
  waiting for transfers between devices: 186 us -> 0 us
  matrix products: 73.4 us -> 0 us
  local copies, waits for them, and re-layouts: 52.8 us -> 2.91 us
  between operations: 13.5 us -> 0.04 us
  other arithmetic: 6.14 us -> 17.9 us
    pallas_call x0 -> x1, Pallas kernels: none -> 347 us  [fused(): pl.pallas_call(fused_kernel, out_shape=jax.ShapeDtypeStruct((rows, width)...]
    all_gather x1 -> x0, blocking collectives: 254 us -> none  [one_chunk(): all_weight = lax.all_gather(row_weight, ('rep', 'tok'), axis=0, tiled=True)]
    reduce_scatter x1 -> x0, waiting for transfers between devices: 185 us -> none  [one_chunk(): lax.psum_scatter(partial.astype(jnp.bfloat16), ('rep', 'tok'), scatter_di...]
    dot_general x3 -> x0, matrix products: 73.4 us -> none  [the longest x1 25.8 us: one_chunk(): u = jnp.dot(everyone, up, preferred_element_type=jnp.float32)]
    dynamic_slice x5 -> x0, local copies, waits for them, and re-layouts: 18.5 us -> none  [the longest x4 18.5 us: reshard_gate_up(): lax.dynamic_index_in_dim(pieces, lax.rem(me + shift, reps), 0, keepdims=F...]
    unnamed x11 -> x1, local copies, waits for them, and re-layouts: 13.7 us -> 1.88 us
    convert_element_type x1 -> x3, other arithmetic: 6.12 us -> 15.2 us  [the longest x1 9.08 us: fused(): gate_up.astype(bf16)]
    transpose x1 -> x0, local copies, waits for them, and re-layouts: 7.54 us -> none  [reshard_gate_up(): pieces = gate_up.astype(jnp.bfloat16).reshape(experts, rows, 2, reps, par...]
  transfers between devices with their start and end apart: 5 -> 0, of which waited for: 1 -> 0; matrix products, arithmetic and copies ran while one was open for 10% -> 0% of each run, Pallas kernels for 0% -> 0%
where the time goes in v2:
time: 370 us; the launch traced here: 368 us
  Pallas kernels  347 us (94%)
  other arithmetic  17.9 us (5%)
    pallas_call x1, Pallas kernels, fused(): pl.pallas_call(fused_kernel, out_shape=jax.ShapeDtypeStruct((rows, width)...  347 us
    convert_element_type x1, other arithmetic, fused(): gate_up.astype(bf16)  9.08 us

profile of v2, /device:TPU:14, one launch (start us, length us, event | category | flops | bytes accessed | tf_op | source)
XLA Modules:
  0.0 368.2 jit_solution(743610161263394498)
XLA Ops:
  0.0 0.1 fusion.4
  0.1 0.7 select_reduce_fusion
  0.8 0.1 copy.11
  0.9 0.1 copy.10
  1.0 0.1 fusion.2
  1.1 0.8 broadcast_in_dim.31.sel_ref
  2.0 1.9 pad_maximum_fusion.x_ref
  3.9 6.0 %convert_element_type.14 = bf16[4,256,2048]{2,1,0:T(8,128)(2,1)} convert(f32[4,256,2048]{2,1,0:T(8,128)} %param.9) | non-fusion elementwise | flops 2097152 | bytes 12582912 | tf_op jit(solution)/shard_map/convert_element_type | solution.py:301
  9.9 9.1 %convert_element_type.13.gate_ref = bf16[4,512,2048]{2,1,0:T(8,128)(2,1)} convert(f32[4,512,2048]{2,1,0:T(8,128)} %param.8) | non-fusion elementwise | flops 4194304 | bytes 25165824 | tf_op jit(solution)/shard_map/convert_element_type | solution.py:301
  19.0 347.3 %shard_map.55 = bf16[128,2048]{1,0:T(8,128)(2,1)} custom-call(bf16[128,2176]{1,0:T(8,128)(2,1)} %pad_maximum_fusion.x_ref, bf16[4,128,256]{2,1,0:T(8,128)(2,1)} %broadcast_in_dim.31.sel_ref, bf16[4,512,2048]{2,1,0:T(8,128)(2,1)} %convert_element_type.13.gate_ref, bf16[1024,2048]{1,0:T(8,128)(2,1)} %bitcast.5), custom_call_target="tpu_custom_call" | custom-call | tf_op jit(solution)/shard_map/pallas_call | solution.py:272
  366.3 1.9 copy.14
  (3 shorter events, 0.0 us)

commit v3 on v2

--- a/solution.py
+++ b/solution.py
@@ -34,9 +34,9 @@
 
 
 def fused_kernel(
-    x_ref, sel_ref, gate_ref, down_ref, out_ref,
-    x, w, d, units, r1, r2, r3, rz,
-    local_sem, w_send, w_recv, z_send, z_recv, ag_send, ag_recv, rs_send, rs_recv, o_send, o_recv,
+    x_ref, sel_ref, gate_ref, down_ref, out_ref, served,
+    x, w, d, units, r1, r2, r3, rz, wide, narrow,
+    local_sem, load_sem, store_sem, w_send, w_recv, z_send, z_recv, ag_send, ag_recv, rs_send, rs_recv, o_send, o_recv,
 ):
     reps, _, _, _, rows, _ = x.shape
     experts, depth, both = w.shape
@@ -53,6 +53,9 @@
     x_mate = {"tok": t + 2 - 4 * xs}
     y_mate = {"tok": t + 4 - 8 * ys}
     rep_mates = [{"rep": lax.rem(r + k, reps)} for k in range(1, reps)]
+    across = reps - 1 - r
+    beside = r + 1 - 2 * lax.rem(r, 2)
+    piece = wide.shape[1]
     other = 1 - core
 
     barrier = pltpu.get_barrier_semaphore()
@@ -74,11 +77,58 @@
         copy.start()
         return copy
 
-    own_x = local(x_ref, x.at[r, ys, xs, core], local_sem.at[0])
-    to_reps = [
-        remote(x_ref, x.at[r, ys, xs, core], z_send.at[k], z_recv.at[k], rep_mates[k])
-        for k in range(reps - 1)
-    ]
+    mine = x.at[r, ys, xs, core]
+    own_x = local(x_ref, mine, local_sem.at[0])
+    from_across = remote(x_ref, mine, z_send.at[0], z_recv.at[0], {"rep": across})
+    from_beside = remote(x_ref, mine, z_send.at[1], z_recv.at[1], {"rep": beside})
+
+    def cast_rows(src, dst_store):
+        def some(n, carry):
+            at = pl.ds(pl.multiple_of(n * 16, 16), 16)
+            dst_store(at, n, src[at, :].astype(jnp.bfloat16))
+            return carry
+
+        lax.fori_loop(0, piece // 16, some, 0)
+
+    def load(source, n):
+        rows_of = pl.ds(n * piece, piece)
+        return local(source.at[rows_of, :], wide.at[n % 2], load_sem.at[n % 2])
+
+    def cast_expert(e):
+        count = gate_ref.shape[1] // piece
+        loads, stores = [load(gate_ref.at[e], 0)], []
+        for n in range(count):
+            if n + 1 < count:
+                loads.append(load(gate_ref.at[e], n + 1))
+            loads[n].wait()
+            if n >= 2:
+                stores[n - 2].wait()
+
+            def keep(at, step, value, slot=n % 2):
+                narrow[slot, at, :] = value
+
+            cast_rows(wide.at[n % 2], keep)
+            stores.append(
+                local(
+                    narrow.at[n % 2], served.at[e, pl.ds(n * piece, piece), :], store_sem.at[n % 2]
+                )
+            )
+        for store in stores[-2:]:
+            store.wait()
+
+    def cast_down():
+        count = d.shape[0] // piece
+        loads = [load(down_ref, 0)]
+        for n in range(count):
+            if n + 1 < count:
+                loads.append(load(down_ref, n + 1))
+            loads[n].wait()
+
+            def keep(at, step, value, base=n * piece):
+                d[pl.ds(pl.multiple_of(base + step * 16, 16), 16), :] = value
+
+            cast_rows(wide.at[n % 2], keep)
+
     landing = pl.ds(pl.multiple_of(r * block_depth, block_depth), block_depth)
 
     def send_weights(e):
@@ -90,40 +140,61 @@
                 columns = pl.ds(pl.multiple_of(half * ff + to * part, part), part)
                 copies.append(
                     remote(
-                        gate_ref.at[e, :, columns], into,
+                        served.at[e, :, columns], into,
                         w_send.at[e, k - 1, half], w_recv.at[e, k - 1, half], rep_mates[k - 1],
                     )
                 )
             columns = pl.ds(pl.multiple_of(half * ff + r * part, part), part)
             copies.append(
-                local(gate_ref.at[e, :, columns], into, local_sem.at[2 + HALVES * e + half])
+                local(served.at[e, :, columns], into, local_sem.at[2 + HALVES * e + half])
             )
         return copies
 
-    weights = [send_weights(e) for e in range(experts - 1)]
-    own_d = local(down_ref, d, local_sem.at[1])
+    cast_expert(0)
+    weights = [send_weights(0)]
+
+    chunk_of = [r, across, beside, reps - 1 - beside]
+    stage = []
+
+    def gather_first(i):
+        block = x.at[chunk_of[i], ys, xs, core]
+        mate = x_mate if i % 2 == 0 else y_mate
+        stage.append(remote(block, block, ag_send.at[i, 0], ag_recv.at[i, 0], mate))
 
     own_x.wait()
-    chunk_of = [lax.rem(r + reps - i, reps) for i in range(reps)]
-    stage = []
-    for i in range(reps):
-        if i:
-            to_reps[i - 1].wait()
-        mine = x.at[chunk_of[i], ys, xs, core]
-        mate = x_mate if i % 2 == 0 else y_mate
-        stage.append(remote(mine, mine, ag_send.at[i, 0], ag_recv.at[i, 0], mate))
+    gather_first(0)
+    cast_expert(1)
+    from_across.wait()
+    block = x.at[across, ys, xs, core]
+    forwarded = remote(block, block, z_send.at[2], z_recv.at[2], {"rep": beside})
+    gather_first(1)
+    from_beside.wait()
+    gather_first(2)
+    weights.append(send_weights(1))
+    forwarded.wait()
+    gather_first(3)
+    cast_expert(2)
     for i in range(reps):
         stage[i].wait()
         if i % 2 == 0:
-            mine, mate = x.at[chunk_of[i], ys, :, core], y_mate
+            block, mate = x.at[chunk_of[i], ys, :, core], y_mate
         else:
-            mine, mate = x.at[chunk_of[i], :, xs, core], x_mate
-        stage[i] = remote(mine, mine, ag_send.at[i, 1], ag_recv.at[i, 1], mate)
+            block, mate = x.at[chunk_of[i], :, xs, core], x_mate
+        stage[i] = remote(block, block, ag_send.at[i, 1], ag_recv.at[i, 1], mate)
+
+    def arrive(e):
+        for copy in weights[e]:
+            copy.wait()
+        if e + 2 < experts:
+            weights.append(send_weights(e + 2))
+
+    arrive(0)
     for i in range(reps):
         stage[i].wait()
-        mine = x.at[chunk_of[i], :, :, core]
-        stage[i] = remote(mine, mine, ag_send.at[i, 2], ag_recv.at[i, 2], core_mate)
-    weights.append(send_weights(experts - 1))
+        block = x.at[chunk_of[i], :, :, core]
+        stage[i] = remote(block, block, ag_send.at[i, 2], ag_recv.at[i, 2], core_mate)
+    cast_expert(3)
+    cast_down()
     for i in range(reps):
         stage[i].wait()
 
@@ -155,19 +226,18 @@
         lax.fori_loop(0, width // step, columns_of, 0)
 
     for e in range(experts - 1):
-        for copy in weights[e]:
-            copy.wait()
+        if e:
+            arrive(e)
 
         def tile(n, carry):
             make_units(e, lax.div(n, 2), lax.rem(n, 2))
             return carry
 
         lax.fori_loop(0, 2 * reps, tile, 0)
-    for copy in weights[experts - 1]:
-        copy.wait()
-    own_d.wait()
+    arrive(experts - 1)
 
     flat = pl.ds(0, width)
+    streams = [pl.ds(q * (width // 2), width // 2) for q in range(2)]
     first, second, third, last = {}, {}, {}, []
 
     def scatter_core(i):
@@ -183,33 +253,40 @@
         first[i].wait_recv()
         project(i, 1)
         c = lax.rem(r + 1 + i, reps)
-        if i % 2 == 0:
-            src, mate = x.at[c, :, 1 - xs, core, :, flat], x_mate
-        else:
-            src, mate = x.at[c, 1 - ys, :, core, :, flat], y_mate
-        second[i] = remote(src, r2.at[i], rs_send.at[i, 1], rs_recv.at[i, 1], mate)
+        for q, columns in enumerate(streams):
+            if q == 0:
+                src, mate = x.at[c, :, 1 - xs, core, :, columns], x_mate
+            else:
+                src, mate = x.at[c, 1 - ys, :, core, :, columns], y_mate
+            second[i, q] = remote(
+                src, r2.at[i, :, :, columns], rs_send.at[i, 1 + q], rs_recv.at[i, 1 + q], mate
+            )
 
     def scatter_third(i):
-        second[i].wait_recv()
-        c = lax.rem(r + 1 + i, reps)
-
-        def add(n, carry):
-            at = pl.ds(pl.multiple_of(n * 16, 16), 16)
-            for k in range(2):
-                where = (c, k, xs, core, at, flat) if i % 2 == 0 else (c, ys, k, core, at, flat)
-                total = x[where].astype(jnp.float32) + r2[i, k, at, :].astype(jnp.float32)
-                x[where] = total.astype(jnp.bfloat16)
-            return carry
-
-        lax.fori_loop(0, rows // 16, add, 0)
-        if i % 2 == 0:
-            src, mate = x.at[c, 1 - ys, xs, core, :, flat], y_mate
-        else:
-            src, mate = x.at[c, ys, 1 - xs, core, :, flat], x_mate
-        third[i] = remote(src, r3.at[i], rs_send.at[i, 2], rs_recv.at[i, 2], mate)
+        c = lax.rem(r + 1 + i, reps)
+        for q, columns in enumerate(streams):
+            second[i, q].wait_recv()
+
+            def add(n, carry, q=q, columns=columns):
+                at = pl.ds(pl.multiple_of(n * 16, 16), 16)
+                for k in range(2):
+                    where = (c, k, xs, core, at, columns) if q == 0 else (c, ys, k, core, at, columns)
+                    total = x[where].astype(jnp.float32) + r2[i, k, at, columns].astype(jnp.float32)
+                    x[where] = total.astype(jnp.bfloat16)
+                return carry
+
+            lax.fori_loop(0, rows // 16, add, 0)
+            if q == 0:
+                src, mate = x.at[c, 1 - ys, xs, core, :, columns], y_mate
+            else:
+                src, mate = x.at[c, ys, 1 - xs, core, :, columns], x_mate
+            third[i, q] = remote(
+                src, r3.at[i, :, columns], rs_send.at[i, 3 + q], rs_recv.at[i, 3 + q], mate
+            )
 
     def scatter_rep(i):
-        third[i].wait_recv()
+        for q in range(2):
+            third[i, q].wait_recv()
         c = lax.rem(r + 1 + i, reps)
         if i == reps - 1:
             return
@@ -271,9 +348,12 @@
     vmem = pl.BlockSpec(memory_space=pltpu.VMEM)
     return pl.pallas_call(
         fused_kernel,
-        out_shape=jax.ShapeDtypeStruct((rows, width), bf16),
+        out_shape=[
+            jax.ShapeDtypeStruct((rows, width), bf16),
+            jax.ShapeDtypeStruct(gate_up.shape, bf16),
+        ],
         in_specs=[hbm, vmem, hbm, hbm],
-        out_specs=vmem,
+        out_specs=[vmem, hbm],
         scratch_shapes=[
             pltpu.VMEM((reps, 2, 2, 2, rows, width + LANES), bf16),
             pltpu.VMEM((experts, depth, 2 * part), bf16),
@@ -283,22 +363,26 @@
             pltpu.VMEM((reps, 2, rows, width), bf16),
             pltpu.VMEM((reps, rows, width), bf16),
             pltpu.VMEM((reps - 1, rows, width), bf16),
+            pltpu.VMEM((2, 128, columns), jnp.float32),
+            pltpu.VMEM((2, 128, columns), bf16),
             dma((2 + HALVES * experts,)),
+            dma((2,)),
+            dma((2,)),
             dma((experts, reps - 1, HALVES)),
             dma((experts, reps - 1, HALVES)),
             dma((reps - 1,)),
             dma((reps - 1,)),
             dma((reps, 3)),
             dma((reps, 3)),
-            dma((reps, 3)),
-            dma((reps, 3)),
+            dma((reps, 5)),
+            dma((reps, 5)),
             dma((reps - 1,)),
             dma((reps - 1,)),
         ],
         compiler_params=pltpu.CompilerParams(
             collective_id=0, has_side_effects=True, vmem_limit_bytes=62 << 20
         ),
-    )(x, sel, gate_up.astype(bf16), down.astype(bf16).reshape(experts * part, width))
+    )(x, sel, gate_up, down.reshape(experts * part, width))[0]
 
 
 def per_device(hidden_states, routes, gate_prob, gate_up, down):
@@ -315,7 +399,8 @@
 
     hit = routes[0][:, :, None] == jnp.arange(all_experts, dtype=jnp.int32)
     weight = jnp.sum(jnp.where(hit, gate_prob[0][:, :, None], 0.0), axis=1)
-    if chunks == 1 and groups == 8 and reps == 4 and 2 * all_experts <= LANES:
+    sizes = (groups, reps, experts, token_count, width, gate_up.shape[1:], down.shape[1])
+    if sizes == (8, 4, 4, 128, 2048, (512, 2048), 256):
         return fused(tokens, weight, gate_up, down, reps)[None]
     gate, up = reshard_gate_up(gate_up, reps)
     stacked_down = down.astype(jnp.bfloat16).reshape(experts * part, width)

time: 370 us -> 312 us (0.84)
  Pallas kernels: 347 us -> 302 us
  other arithmetic: 17.9 us -> 2.86 us
    pallas_call x1, Pallas kernels: 347 us -> 302 us  [fused(): pl.pallas_call(fused_kernel, out_shape=[jax.ShapeDtypeStruct((rows, width...]
    convert_element_type x2 -> x0, other arithmetic: 15.1 us -> none  [the longest x1 9.08 us: fused(): gate_up.astype(bf16)]
where the time goes in v3:
time: 312 us; the launch traced here: 308 us
  Pallas kernels  302 us (97%)
    pallas_call x1, Pallas kernels, fused(): pl.pallas_call(fused_kernel, out_shape=[jax.ShapeDtypeStruct((rows, width...  302 us

profile of v3, /device:TPU:14, one launch (start us, length us, event | category | flops | bytes accessed | tf_op | source)
XLA Modules:
  0.0 307.7 jit_solution(6265754384032754450)
XLA Ops:
  0.0 0.1 fusion.4
  0.1 0.7 select_reduce_fusion
  0.8 0.1 copy.11
  0.9 0.1 copy.10
  1.0 0.1 fusion.2
  1.1 0.8 broadcast_in_dim.31.sel_ref
  2.0 1.9 pad_maximum_fusion.x_ref
  3.9 301.9 %shard_map.55 = (bf16[128,2048]{1,0:T(8,128)(2,1)}, bf16[4,512,2048]{2,1,0:T(8,128)(2,1)}) custom-call(bf16[128,2176]{1,0:T(8,128)(2,1)} %pad_maximum_fusion.x_ref, bf16[4,128,256]{2,1,0:T(8,128)(2,1)} %broadcast_in_dim.31.sel_ref, f32[4,512,2048]{2,1,0:T(8,128)} %gate_ref.1, f32[1024,2048]{1,0:T(8,128)} %bitcast.5), custom_call_target="tpu_custom_call" | custom-call | tf_op jit(solution)/shard_map/pallas_call | solution.py:349
  305.8 1.9 copy.14
  (3 shorter events, 0.0 us)

commit v4 on v3

--- a/solution.py
+++ b/solution.py
@@ -209,21 +209,47 @@
         unit = g * (1.0 / (1.0 + jnp.exp(-g))) * u * scale
         units[i, half, :, pl.ds(e * part, part)] = unit.astype(jnp.bfloat16)
 
-    def project(i, half):
+    step = 512
+    spent = (experts - 1) * part
+    ahead = {(0, 0): 0, (0, 1): 1, (1, 0): 2}
+
+    def project_ahead(i, half):
+        slot = ahead[i, half]
+
+        def columns_of(n, carry):
+            at = pl.ds(pl.multiple_of(n * step, step), step)
+            total = jnp.dot(
+                units[i, half, :, pl.ds(0, spent)], d[pl.ds(0, spent), at],
+                preferred_element_type=jnp.float32,
+            )
+            w[slot, at, :] = total.astype(jnp.bfloat16)
+            return carry
+
+        lax.fori_loop(0, width // step, columns_of, 0)
+
+    def project(i, half, q):
         c = lax.rem(r + 1 + i, reps)
         h = other if half == 0 else core
-        step = 512
+        slot = ahead.get((i, half))
+        below = 0 if slot is None else spent
+        depth_of = pl.ds(below, d.shape[0] - below)
+        count = width // step // 2
 
         def columns_of(n, carry):
             columns = pl.ds(pl.multiple_of(n * step, step), step)
-            total = jnp.dot(units[i, half], d[:, columns], preferred_element_type=jnp.float32)
+            total = jnp.dot(
+                units[i, half, :, depth_of], d[depth_of, columns],
+                preferred_element_type=jnp.float32,
+            )
+            if slot is not None:
+                total = total + w[slot, columns, :].astype(jnp.float32)
             total = total.reshape(2, 2, rows, step)
             if half:
                 total = total + r1[i, :, :, :, columns].astype(jnp.float32)
             x[c, :, :, h, :, columns] = total.astype(jnp.bfloat16)
             return carry
 
-        lax.fori_loop(0, width // step, columns_of, 0)
+        lax.fori_loop(q * count, (q + 1) * count, columns_of, 0)
 
     for e in range(experts - 1):
         if e:
@@ -234,6 +260,8 @@
             return carry
 
         lax.fori_loop(0, 2 * reps, tile, 0)
+    for i, half in ahead:
+        project_ahead(i, half)
     arrive(experts - 1)
 
     flat = pl.ds(0, width)
@@ -242,24 +270,26 @@
 
     def scatter_core(i):
         make_units(experts - 1, i, 0)
-        project(i, 0)
-        c = lax.rem(r + 1 + i, reps)
-        first[i] = remote(
-            x.at[c, :, :, other, :, flat], r1.at[i], rs_send.at[i, 0], rs_recv.at[i, 0], core_mate
-        )
+        c = lax.rem(r + 1 + i, reps)
+        for q, columns in enumerate(streams):
+            project(i, 0, q)
+            first[i, q] = remote(
+                x.at[c, :, :, other, :, columns], r1.at[i, :, :, :, columns],
+                rs_send.at[i, q], rs_recv.at[i, q], core_mate,
+            )
 
     def scatter_second(i):
         make_units(experts - 1, i, 1)
-        first[i].wait_recv()
-        project(i, 1)
         c = lax.rem(r + 1 + i, reps)
         for q, columns in enumerate(streams):
+            first[i, q].wait_recv()
+            project(i, 1, q)
             if q == 0:
                 src, mate = x.at[c, :, 1 - xs, core, :, columns], x_mate
             else:
                 src, mate = x.at[c, 1 - ys, :, core, :, columns], y_mate
             second[i, q] = remote(
-                src, r2.at[i, :, :, columns], rs_send.at[i, 1 + q], rs_recv.at[i, 1 + q], mate
+                src, r2.at[i, :, :, columns], rs_send.at[i, 2 + q], rs_recv.at[i, 2 + q], mate
             )
 
     def scatter_third(i):
@@ -281,7 +311,7 @@
             else:
                 src, mate = x.at[c, ys, 1 - xs, core, :, columns], x_mate
             third[i, q] = remote(
-                src, r3.at[i, :, columns], rs_send.at[i, 3 + q], rs_recv.at[i, 3 + q], mate
+                src, r3.at[i, :, columns], rs_send.at[i, 4 + q], rs_recv.at[i, 4 + q], mate
             )
 
     def scatter_rep(i):
@@ -305,12 +335,14 @@
             )
         )
 
-    for step in range(reps + 3):
-        if step < reps:
-            scatter_core(step)
-        for lag, work in ((1, scatter_second), (2, scatter_third), (3, scatter_rep)):
-            if 0 <= step - lag < reps:
-                work(step - lag)
+    order = [
+        (scatter_core, 0), (scatter_second, 0), (scatter_core, 1), (scatter_core, 2),
+        (scatter_second, 1), (scatter_core, 3), (scatter_second, 2), (scatter_third, 0),
+        (scatter_second, 3), (scatter_third, 1), (scatter_rep, 0), (scatter_third, 2),
+        (scatter_rep, 1), (scatter_third, 3), (scatter_rep, 2), (scatter_rep, 3),
+    ]
+    for work, i in order:
+        work(i)
     for copy in last:
         copy.wait_recv()
 
@@ -374,8 +406,8 @@
             dma((reps - 1,)),
             dma((reps, 3)),
             dma((reps, 3)),
-            dma((reps, 5)),
-            dma((reps, 5)),
+            dma((reps, 6)),
+            dma((reps, 6)),
             dma((reps - 1,)),
             dma((reps - 1,)),
         ],

time: 312 us -> 318 us (1.019)
  Pallas kernels: 302 us -> 309 us
    pallas_call x1, Pallas kernels: 302 us -> 309 us  [fused(): pl.pallas_call(fused_kernel, out_shape=[jax.ShapeDtypeStruct((rows, width...]
where the time goes in v4:
time: 318 us; the launch traced here: 315 us
  Pallas kernels  309 us (97%)
    pallas_call x1, Pallas kernels, fused(): pl.pallas_call(fused_kernel, out_shape=[jax.ShapeDtypeStruct((rows, width...  309 us

profile of v4, /device:TPU:14, one launch (start us, length us, event | category | flops | bytes accessed | tf_op | source)
XLA Modules:
  0.0 314.9 jit_solution(14234557040836364246)
XLA Ops:
  0.0 0.1 fusion.4
  0.1 0.7 select_reduce_fusion
  0.8 0.1 copy.11
  0.9 0.1 copy.10
  1.0 0.1 fusion.2
  1.1 0.8 broadcast_in_dim.31.sel_ref
  2.0 1.9 pad_maximum_fusion.x_ref
  3.9 309.1 %shard_map.55 = (bf16[128,2048]{1,0:T(8,128)(2,1)}, bf16[4,512,2048]{2,1,0:T(8,128)(2,1)}) custom-call(bf16[128,2176]{1,0:T(8,128)(2,1)} %pad_maximum_fusion.x_ref, bf16[4,128,256]{2,1,0:T(8,128)(2,1)} %broadcast_in_dim.31.sel_ref, f32[4,512,2048]{2,1,0:T(8,128)} %gate_ref.1, f32[1024,2048]{1,0:T(8,128)} %bitcast.5), custom_call_target="tpu_custom_call" | custom-call | tf_op jit(solution)/shard_map/pallas_call | solution.py:381
  313.0 1.9 copy.14
  (3 shorter events, 0.0 us)

commit v5 on v4

--- a/solution.py
+++ b/solution.py
@@ -151,15 +151,34 @@
         return copies
 
     cast_expert(0)
-    weights = [send_weights(0)]
 
     chunk_of = [r, across, beside, reps - 1 - beside]
-    stage = []
+    stage = [None] * reps
+    weights = []
 
     def gather_first(i):
         block = x.at[chunk_of[i], ys, xs, core]
         mate = x_mate if i % 2 == 0 else y_mate
-        stage.append(remote(block, block, ag_send.at[i, 0], ag_recv.at[i, 0], mate))
+        stage[i] = remote(block, block, ag_send.at[i, 0], ag_recv.at[i, 0], mate)
+
+    def gather_second(i):
+        stage[i].wait()
+        if i % 2 == 0:
+            block, mate = x.at[chunk_of[i], ys, :, core], y_mate
+        else:
+            block, mate = x.at[chunk_of[i], :, xs, core], x_mate
+        stage[i] = remote(block, block, ag_send.at[i, 1], ag_recv.at[i, 1], mate)
+
+    def gather_core(i):
+        stage[i].wait()
+        block = x.at[chunk_of[i], :, :, core]
+        stage[i] = remote(block, block, ag_send.at[i, 2], ag_recv.at[i, 2], core_mate)
+
+    def arrive(e):
+        for copy in weights[e]:
+            copy.wait()
+        if e + 2 < experts:
+            weights.append(send_weights(e + 2))
 
     own_x.wait()
     gather_first(0)
@@ -167,36 +186,23 @@
     from_across.wait()
     block = x.at[across, ys, xs, core]
     forwarded = remote(block, block, z_send.at[2], z_recv.at[2], {"rep": beside})
+    weights.append(send_weights(0))
     gather_first(1)
     from_beside.wait()
     gather_first(2)
+    for i in range(reps - 1):
+        gather_second(i)
     weights.append(send_weights(1))
+    cast_expert(2)
     forwarded.wait()
     gather_first(3)
-    cast_expert(2)
-    for i in range(reps):
-        stage[i].wait()
-        if i % 2 == 0:
-            block, mate = x.at[chunk_of[i], ys, :, core], y_mate
-        else:
-            block, mate = x.at[chunk_of[i], :, xs, core], x_mate
-        stage[i] = remote(block, block, ag_send.at[i, 1], ag_recv.at[i, 1], mate)
-
-    def arrive(e):
-        for copy in weights[e]:
-            copy.wait()
-        if e + 2 < experts:
-            weights.append(send_weights(e + 2))
-
+    for i in range(reps - 1):
+        gather_core(i)
     arrive(0)
-    for i in range(reps):
-        stage[i].wait()
-        block = x.at[chunk_of[i], :, :, core]
-        stage[i] = remote(block, block, ag_send.at[i, 2], ag_recv.at[i, 2], core_mate)
+    gather_second(3)
     cast_expert(3)
+    gather_core(3)
     cast_down()
-    for i in range(reps):
-        stage[i].wait()
 
     def make_units(e, i, half):
         c = lax.rem(r + 1 + i, reps)
@@ -211,7 +217,7 @@
 
     step = 512
     spent = (experts - 1) * part
-    ahead = {(0, 0): 0, (0, 1): 1, (1, 0): 2}
+    ahead = {(0, 0): 0, (1, 0): 1, (2, 0): 2}
 
     def project_ahead(i, half):
         slot = ahead[i, half]
@@ -251,11 +257,19 @@
 
         lax.fori_loop(q * count, (q + 1) * count, columns_of, 0)
 
-    for e in range(experts - 1):
-        if e:
-            arrive(e)
-
-        def tile(n, carry):
+    for i in range(reps):
+        stage[i].wait()
+        place = lax.rem(chunk_of[i] + 2 * reps - r - 1, reps)
+
+        def half_tile(half, carry, place=place):
+            make_units(0, place, half)
+            return carry
+
+        lax.fori_loop(0, 2, half_tile, 0)
+    for e in range(1, experts - 1):
+        arrive(e)
+
+        def tile(n, carry, e=e):
             make_units(e, lax.div(n, 2), lax.rem(n, 2))
             return carry
 
@@ -336,8 +350,8 @@
         )
 
     order = [
-        (scatter_core, 0), (scatter_second, 0), (scatter_core, 1), (scatter_core, 2),
-        (scatter_second, 1), (scatter_core, 3), (scatter_second, 2), (scatter_third, 0),
+        (scatter_core, 0), (scatter_core, 1), (scatter_core, 2), (scatter_second, 0),
+        (scatter_core, 3), (scatter_second, 1), (scatter_second, 2), (scatter_third, 0),
         (scatter_second, 3), (scatter_third, 1), (scatter_rep, 0), (scatter_third, 2),
         (scatter_rep, 1), (scatter_third, 3), (scatter_rep, 2), (scatter_rep, 3),
     ]

time: 318 us -> 320 us (level)
  Pallas kernels: 309 us -> 313 us
    pallas_call x1, Pallas kernels: 309 us -> 313 us  [fused(): pl.pallas_call(fused_kernel, out_shape=[jax.ShapeDtypeStruct((rows, width...]
where the time goes in v5:
time: 320 us; the launch traced here: 319 us
  Pallas kernels  313 us (98%)
    pallas_call x1, Pallas kernels, fused(): pl.pallas_call(fused_kernel, out_shape=[jax.ShapeDtypeStruct((rows, width...  313 us

profile of v5, /device:TPU:14, one launch (start us, length us, event | category | flops | bytes accessed | tf_op | source)
XLA Modules:
  0.0 318.7 jit_solution(11468136322994732951)
XLA Ops:
  0.0 0.1 fusion.4
  0.1 0.7 select_reduce_fusion
  0.8 0.1 copy.11
  0.9 0.1 copy.10
  1.0 0.1 fusion.2
  1.1 0.8 broadcast_in_dim.31.sel_ref
  2.0 1.9 pad_maximum_fusion.x_ref
  3.9 312.9 %shard_map.55 = (bf16[128,2048]{1,0:T(8,128)(2,1)}, bf16[4,512,2048]{2,1,0:T(8,128)(2,1)}) custom-call(bf16[128,2176]{1,0:T(8,128)(2,1)} %pad_maximum_fusion.x_ref, bf16[4,128,256]{2,1,0:T(8,128)(2,1)} %broadcast_in_dim.31.sel_ref, f32[4,512,2048]{2,1,0:T(8,128)} %gate_ref.1, f32[1024,2048]{1,0:T(8,128)} %bitcast.5), custom_call_target="tpu_custom_call" | custom-call | tf_op jit(solution)/shard_map/pallas_call | solution.py:395
  316.8 1.9 copy.14
  (3 shorter events, 0.0 us)

commit v6 on v3

--- a/solution.py
+++ b/solution.py
@@ -164,13 +164,13 @@
     own_x.wait()
     gather_first(0)
     cast_expert(1)
+    weights.append(send_weights(1))
     from_across.wait()
     block = x.at[across, ys, xs, core]
     forwarded = remote(block, block, z_send.at[2], z_recv.at[2], {"rep": beside})
     gather_first(1)
     from_beside.wait()
     gather_first(2)
-    weights.append(send_weights(1))
     forwarded.wait()
     gather_first(3)
     cast_expert(2)

time: 312 us -> 340 us (1.090)
  Pallas kernels: 302 us -> 330 us
    pallas_call x1, Pallas kernels: 302 us -> 330 us  [fused(): pl.pallas_call(fused_kernel, out_shape=[jax.ShapeDtypeStruct((rows, width...]
where the time goes in v6:
time: 340 us; the launch traced here: 336 us
  Pallas kernels  330 us (97%)
    pallas_call x1, Pallas kernels, fused(): pl.pallas_call(fused_kernel, out_shape=[jax.ShapeDtypeStruct((rows, width...  330 us

profile of v6, /device:TPU:14, one launch (start us, length us, event | category | flops | bytes accessed | tf_op | source)
XLA Modules:
  0.0 336.0 jit_solution(8603776724616909627)
XLA Ops:
  0.0 0.1 fusion.4
  0.1 0.7 select_reduce_fusion
  0.8 0.1 copy.11
  0.9 0.1 copy.10
  1.0 0.1 fusion.2
  1.1 0.8 broadcast_in_dim.31.sel_ref
  2.0 1.9 pad_maximum_fusion.x_ref
  3.9 330.2 %shard_map.55 = (bf16[128,2048]{1,0:T(8,128)(2,1)}, bf16[4,512,2048]{2,1,0:T(8,128)(2,1)}) custom-call(bf16[128,2176]{1,0:T(8,128)(2,1)} %pad_maximum_fusion.x_ref, bf16[4,128,256]{2,1,0:T(8,128)(2,1)} %broadcast_in_dim.31.sel_ref, f32[4,512,2048]{2,1,0:T(8,128)} %gate_ref.1, f32[1024,2048]{1,0:T(8,128)} %bitcast.5), custom_call_target="tpu_custom_call" | custom-call | tf_op jit(solution)/shard_map/pallas_call | solution.py:349
  334.1 1.9 copy.14
  (3 shorter events, 0.0 us)
